TPU v7x, 32 devices: a whole 2x2x4 slice. The times are simulated.
32 devices in a mesh: group: 2 (over x), tm: 16 (over z, y, core).
Axes of the slice: x: 2, y: 2, z: 4, core: 2. Of those that a mesh axis runs over, the one named last changes fastest.
Arguments:
- obs_blocks: bfloat16 [32, 512, 64, 128], P(('group', 'tm')), parts along dimension 0, may hold values from -0.5 to 0.5
- block_rows: int32 [32, 512], P(('group', 'tm')), parts along dimension 0, may hold values from 0 to 511
- block_cols: int32 [32, 512], P(('group', 'tm')), parts along dimension 0, may hold values from 0 to 15
- block_count: int32 [32], P(('group', 'tm')), parts along dimension 0, may hold values from 256 to 512, as said below
- background: bfloat16 [32, 16, 2048], P(('group', 'tm')), parts along dimension 0, may hold values from -6 to 6
- observed: float32 [32, 16, 32768], P(('group', 'tm')), parts along dimension 0, may hold values from -6 to 6
- obs_weight: float32 [32, 32768], P(('group', 'tm')), parts along dimension 0, may hold values from 0.01 to 0.1
- info_diag: float32 [32, 2048], P(('group', 'tm')), parts along dimension 0, may hold values from 0.003 to 0.03
- decay: float32 [32, 2048], P(('group', 'tm')), parts along dimension 0, may hold values from 0.5 to 1
- noise_var: float32 [32, 2048], P(('group', 'tm')), parts along dimension 0, may hold values from 0.003 to 0.03
- prior_var: float32 [4096], P('group'), parts along dimension 0, may hold values from 0.5 to 2
Outputs:
- smooth_mean: float32 [32, 16, 2048], P(('group', 'tm')), parts along dimension 0
- smooth_var: float32 [32, 2048], P(('group', 'tm')), parts along dimension 0
There are 2 independent parts, one for each index of `group`. A program takes and returns all parts, laid end to end along the dimension named above; each array names one. Nothing has to cross between parts.
Inputs may be any that keep to these rules, and one draw needn't show every extreme that they name: Blocks 0 to block_count[t] - 1 of step t are in use; some step uses all 512 blocks and some step exactly half of them.
All inputs are finite; a program needn't handle non-finite values.
Results may differ from a plain program's by a relative error of at most 0.0045.
Values sent between devices are 32-bit elements; how exact they have to be, the bound alone decides.
A program may use at most 64 MiB of HBM per device.

v0:
```python
import jax
import jax.numpy as jnp
from jax import lax
from jax.sharding import PartitionSpec as P


def split_path(onehot, values, form):
    high_part = values.astype(jnp.bfloat16)
    rest_part = (values - high_part.astype(jnp.float32)).astype(jnp.bfloat16)
    first = jnp.einsum(form, onehot, high_part, preferred_element_type=jnp.float32)
    return first + jnp.einsum(form, onehot, rest_part, preferred_element_type=jnp.float32)


def gradients(obs_blocks, block_rows, block_cols, block_count, background, observed, obs_weight):
    step_total, block_total, row_size, col_size = obs_blocks.shape
    member_total = background.shape[1]
    group_total = background.shape[2] // col_size
    row_total = observed.shape[2] // row_size
    active = lax.broadcasted_iota(jnp.int32, (step_total, block_total), 1) < block_count[:, None]
    col_match = (
        block_cols[:, :, None]
        == lax.broadcasted_iota(jnp.int32, (step_total, block_total, group_total), 2)
    ).astype(jnp.bfloat16)
    row_match = block_rows[:, :, None] == lax.broadcasted_iota(
        jnp.int32, (step_total, block_total, row_total), 2
    )
    row_indicator = jnp.logical_and(row_match, active[:, :, None]).astype(jnp.bfloat16)
    states = background.reshape(step_total, member_total, group_total, col_size)
    picked = jnp.einsum(
        "sbk,smkc->smbc", col_match, states, preferred_element_type=jnp.float32
    ).astype(jnp.bfloat16)
    applied_result = jnp.einsum(
        "sbic,smbc->smbi", obs_blocks, picked, preferred_element_type=jnp.float32
    )
    mapped_images = split_path(row_indicator, applied_result, "dez,dwet->dwzt")
    misfit = observed - mapped_images.reshape(step_total, member_total, row_total * row_size)
    weighted = (obs_weight[:, None, :] * misfit).reshape(
        step_total, member_total, row_total, row_size
    )
    rows_back = jnp.einsum(
        "ocd,owdh->owch",
        row_indicator,
        weighted.astype(jnp.bfloat16),
        preferred_element_type=jnp.float32,
    ).astype(jnp.bfloat16)
    pulled = jnp.einsum(
        "sbic,smbi->smbc", obs_blocks, rows_back, preferred_element_type=jnp.float32
    )
    gradient = split_path(col_match, pulled, "sbk,smbc->smkc")
    return gradient.reshape(step_total, member_total, group_total * col_size)


def sequential_smoother(series, prior_here, member_total):
    full_steps = series.shape[0]
    grad_all = series[:, :member_total, :]
    info_all = series[:, member_total, :]
    decay_all = series[:, member_total + 1, :]
    noise_all = series[:, member_total + 2, :]
    local_width = series.shape[2]
    step_ids = jnp.arange(full_steps)
    first_flags = step_ids == 0
    final_flags = step_ids == full_steps - 1

    def forward(carried, inputs):
        mean_prev, var_prev = carried
        grad_now, info_now, decay_now, noise_now, first_now = inputs
        pred_var = jnp.where(first_now, prior_here, decay_now * decay_now * var_prev + noise_now)
        pred_mean = jnp.where(first_now, 0.0, decay_now * mean_prev)
        var_now = pred_var / (1.0 + info_now * pred_var)
        mean_now = var_now * (pred_mean / pred_var + grad_now)
        return ((mean_now, var_now), (mean_now, var_now))

    initial = (
        jnp.zeros((member_total, local_width), jnp.float32),
        jnp.ones((local_width,), jnp.float32),
    )
    means, variances = lax.scan(
        forward, initial, (grad_all, info_all, decay_all, noise_all, first_flags)
    )[1]
    next_decay = jnp.concatenate([decay_all[1:], jnp.zeros((1, local_width), jnp.float32)], axis=0)
    next_noise = jnp.concatenate([noise_all[1:], jnp.ones((1, local_width), jnp.float32)], axis=0)

    def backward(carried, inputs):
        later_mean, later_var = carried
        mean_now, var_now, decay_next, noise_next, final_now = inputs
        pred_var = decay_next * decay_next * var_now + noise_next
        smoother_gain = jnp.where(final_now, 0.0, var_now * decay_next / pred_var)
        out_mean = mean_now + smoother_gain * (later_mean - decay_next * mean_now)
        out_var = var_now + smoother_gain * smoother_gain * (later_var - pred_var)
        return ((out_mean, out_var), (out_mean, out_var))

    closing = (
        jnp.zeros((member_total, local_width), jnp.float32),
        jnp.zeros((local_width,), jnp.float32),
    )
    return lax.scan(
        backward, closing, (means, variances, next_decay, next_noise, final_flags), reverse=True
    )[1]


def shards(
    obs_blocks,
    block_rows,
    block_cols,
    block_count,
    background,
    observed,
    obs_weight,
    info_diag,
    decay,
    noise_var,
    prior_var,
):
    member_total = background.shape[1]
    state_total = background.shape[2]
    gradient = gradients(
        obs_blocks, block_rows, block_cols, block_count, background, observed, obs_weight
    )
    packed = jnp.concatenate(
        [gradient, info_diag[:, None, :], decay[:, None, :], noise_var[:, None, :]], axis=1
    )
    series = lax.all_to_all(packed, "tm", split_axis=2, concat_axis=0, tiled=True)
    local_width = state_total // lax.axis_size("tm")
    prior_here = lax.dynamic_slice_in_dim(
        prior_var, lax.axis_index("tm") * local_width, local_width, 0
    )
    mean_series, var_series = sequential_smoother(series, prior_here, member_total)
    outgoing = jnp.concatenate([mean_series, var_series[:, None, :]], axis=1)
    returned = lax.all_to_all(outgoing, "tm", split_axis=0, concat_axis=2, tiled=True)
    return (returned[:, :member_total, :], returned[:, member_total, :])


def solution(mesh):
    in_specs = (
        P(("group", "tm"), None, None, None),
        P(("group", "tm"), None),
        P(("group", "tm"), None),
        P(("group", "tm")),
        P(("group", "tm"), None, None),
        P(("group", "tm"), None, None),
        P(("group", "tm"), None),
        P(("group", "tm"), None),
        P(("group", "tm"), None),
        P(("group", "tm"), None),
        P("group"),
    )
    out_specs = (P(("group", "tm"), None, None), P(("group", "tm"), None))
    return jax.shard_map(shards, mesh=mesh, in_specs=in_specs, out_specs=out_specs, check_vma=False)
```

profile of v0, /device:TPU:0, one launch (start us, length us, event | category | flops | bytes accessed | tf_op | source)
XLA Modules:
  0.0 153.4 jit_solution(15889140871200153109)
XLA Ops:
  0.6 0.9 copy.100
  1.5 1.4 convert_bitcast_fusion
  2.9 7.2 %fusion.23 = f32[512,16,64]{2,1,0:T(8,128)S(1)} fusion(bf16[1,512,64,128]{3,2,1,0:T(8,128)(2,1)} %param.15, bf16[16,512,128]{2,1,0:T(8,128)(2,1)S(1)} %convert_bitcast_fusion), kind=kOutput, calls=%fused_computation.44 | convolution fusion | flops 134217728 | bytes 12582912 | tf_op jit(solution)/shard_map/sbic,smbc->smbi/dot_general | solution.py:32
  11.5 1.0 fusion.33
  12.5 1.1 add_bitcast_fusion
  13.6 2.7 %copy.84 = f32[1,16,512,64]{3,2,1,0:T(8,128)} copy(f32[1,16,512,64]{2,3,1,0:T(8,128)S(1)} %add_bitcast_fusion) | data formatting | bytes 4194304 | tf_op jit(solution)/shard_map/add | solution.py:11
  16.3 2.9 %reshape.249 = f32[1,16,32768]{2,1,0:T(8,128)S(1)} reshape(f32[1,16,512,64]{3,2,1,0:T(8,128)} %copy.84) | data formatting | bytes 4194304 | tf_op jit(solution)/shard_map/reshape | solution.py:36
  19.3 1.8 %multiply_convert_fusion = bf16[1,16,32768]{2,1,0:T(8,128)(2,1)S(1)} fusion(f32[1,16,32768]{2,1,0:T(8,128)} %param.20, f32[1,16,32768]{2,1,0:T(8,128)S(1)} %reshape.249, f32[32768]{0:T(1024)S(1)} %bitcast.211), kind=kLoop, calls=%fused_computation.63 | loop fusion | flops 1572864 | bytes 5373952 | tf_op jit(solution)/shard_map/convert_element_type | solution.py:43
  21.1 2.3 %convert_element_type.58 = bf16[16,512,64]{2,1,0:T(8,128)(2,1)S(1)} reshape(bf16[1,16,32768]{2,1,0:T(8,128)(2,1)S(1)} %multiply_convert_fusion) | data formatting | bytes 2097152 | tf_op jit(solution)/shard_map/convert_element_type | solution.py:43
  23.4 1.5 fusion.40
  24.9 2.0 %copy.86 = bf16[16,512,64]{2,0,1:T(8,128)(2,1)S(1)} copy(bf16[16,512,64]{1,2,0:T(8,128)(2,1)S(1)} %fusion.40) | data formatting | bytes 2097152 | tf_op jit(solution)/shard_map/reshape.26
  26.9 4.7 %fusion.21 = f32[512,16,128]{2,1,0:T(8,128)S(1)} fusion(bf16[16,512,64]{2,0,1:T(8,128)(2,1)S(1)} %copy.86, bf16[1,512,64,128]{3,2,1,0:T(8,128)(2,1)} %param.15), kind=kOutput, calls=%fused_computation.42 | convolution fusion | flops 134217728 | bytes 13631488 | tf_op jit(solution)/shard_map/sbic,smbi->smbc/dot_general | solution.py:46
  34.4 1.9 %copy.91 = f32[1,1,2048]{1,0,2:T(1,128)} copy(f32[1,1,2048]{2,1,0:T(1,128)S(1)} %bitcast.217) | data formatting | bytes 16384 | tf_op jit(solution)/shard_map/broadcast_in_dim | solution.py:120
  36.3 1.9 %copy.92 = f32[1,1,2048]{1,0,2:T(1,128)} copy(f32[1,1,2048]{2,1,0:T(1,128)S(1)} %bitcast.218) | data formatting | bytes 16384 | tf_op jit(solution)/shard_map/broadcast_in_dim | solution.py:120
  38.2 7.8 %fusion.69 = f32[2048,1,19]{2,1,0:T(1,128)S(1)} fusion(f32[1,1,2048]{1,0,2:T(1,128)} %copy.92, f32[1,1,2048]{1,0,2:T(1,128)} %copy.91, f32[1,1,2048]{1,0,2:T(1,128)S(1)} %copy.90, f32[1,16,2048]{1,0,2:T(1,128)S(1)} %bitcast.203), kind=kLoop, calls=%fused_computation.97 | loop fusion | flops 116736 | bytes 311296
  46.6 9.3 %reduce = f32[2048,19]{1,0:T(8,128)S(1)} reduce(f32[2048,1,19]{2,1,0:T(1,128)S(1)} %fusion.69, f32[]{:T(128)} %broadcast.158), dimensions={1}, to_apply=%fusion.69.reduce_sub_computation | reduce | bytes 311300
  55.8 1.5 reshape.256
  57.4 7.4 %all-to-all-start = ((f32[16,1,2432]{2,1,0:T(1,128)}), f32[16,1,2432]{2,1,0:T(1,128)S(1)}, u32[]{:S(2)}, u32[]{:S(2)}) async-start(f32[16,1,2432]{2,1,0:T(1,128)} %reshape.256), calls=%async_computation | async-start | bytes 311296 | tf_op jit(solution)/shard_map/all_to_all | solution.py:122
  65.6 7.5 %all-to-all-done = f32[16,1,2432]{2,1,0:T(1,128)S(1)} async-done(((f32[16,1,2432]{2,1,0:T(1,128)}), f32[16,1,2432]{2,1,0:T(1,128)S(1)}, u32[]{:S(2)}, u32[]{:S(2)}) %all-to-all-start) | async-done | bytes 155680 | tf_op jit(solution)/shard_map/all_to_all | solution.py:122
  73.1 0.9 reduce.1
  74.0 1.7 %reshape.257 = f32[2048,1,19]{2,1,0:T(1,128)S(1)} reshape(f32[16,2432]{1,0:T(8,128)S(1)} %reduce.1) | data formatting | bytes 311296
  76.4 31.9 %while.38 = (s32[]{:T(128)}, f32[16,128]{1,0:T(8,128)S(1)}, f32[128]{0:T(128)S(1)}, f32[16,16,128]{2,1,0:T(8,128)S(1)}, f32[16,128]{1,0:T(8,128)S(1)}, /*index=5...) while((s32[]{:T(128)}, f32[16,128]{1,0:T(8,128)S(1)}, ...), condition=%wide.region_1.2_spmd.clone, body=%wide.region_0.1_spmd.clone.sunk | while | flops 13315 | bytes 55968 | solution.py:77
  108.3 32.1 %while.39 = (s32[]{:T(128)}, f32[16,128]{1,0:T(8,128)S(1)}, f32[128]{0:T(128)S(1)}, f32[16,16,128]{2,1,0:T(8,128)S(1)}, f32[16,128]{1,0:T(8,128)S(1)}, /*index=5...) while((s32[]{:T(128)}, f32[16,128]{1,0:T(8,128)S(1)}, ...), condition=%wide.region_3.4_spmd.clone, body=%wide.region_2.3_spmd.clone.sunk | while | flops 12420 | bytes 40108 | solution.py:96
  140.4 11.6 %all_to_all.36 = f32[16,17,128]{2,1,0:T(8,128)S(1)} all-to-all(f32[16,17,128]{2,1,0:T(8,128)S(1)} %pad_maximum_fusion.1), channel_id=1, replica_groups=mesh['group'=2,'tm'=16] {'tm'}, dimensions={0} | all-to-all | bytes 278528 | tf_op jit(solution)/shard_map/all_to_all | solution.py:129
  (204 shorter events, 69.6 us)
Async XLA Ops:
  10.5 1.0 copy-start.4
  16.3 3.0 %copy-start = (f32[1,32768]{1,0:T(1,128)S(1)}, f32[1,32768]{1,0:T(1,128)}, u32[]{:S(2)}) copy-start(f32[1,32768]{1,0:T(1,128)} %param.21) | copy-start | bytes 393220
  31.9 0.7 copy-start.5
  33.0 0.8 copy-start.1
  33.0 1.4 copy-start.2
  33.4 2.9 %copy-start.3 = (f32[1,2048]{1,0:T(1,128)S(1)}, f32[1,2048]{1,0:T(1,128)}, u32[]{:S(2)}) copy-start(f32[1,2048]{1,0:T(1,128)} %param.24) | copy-start | bytes 24580
  57.4 15.7 %all-to-all-start = ((f32[16,1,2432]{2,1,0:T(1,128)}), f32[16,1,2432]{2,1,0:T(1,128)S(1)}, u32[]{:S(2)}, u32[]{:S(2)}) async-start(f32[16,1,2432]{2,1,0:T(1,128)} %reshape.256), calls=%async_computation | async-start | bytes 311296 | tf_op jit(solution)/shard_map/all_to_all | solution.py:122
where the time goes:
time: 154 us; the launch traced here: 153 us
  other arithmetic  63.4 us (41%)
  local copies, waits for them, and re-layouts  43.1 us (28%)
  matrix products  17.7 us (11%)
  blocking collectives  11.6 us (8%)
  waiting for transfers between devices  7.51 us (5%)
  starting transfers between devices  7.39 us (5%)
  between operations  1.64 us (1%)
    dynamic_slice x48, local copies, waits for them, and re-layouts, sequential_smoother(): lax.scan(forward, initial, (grad_all, info_all, decay_all, noise_all, fir...  19.5 us
    unnamed x6, other arithmetic  17.1 us
    all_to_all x1, blocking collectives, shards(): lax.all_to_all(outgoing, 'tm', split_axis=0, concat_axis=2, tiled=True)  11.6 us
    add x16, other arithmetic, backward(): out_var = var_now + smoother_gain * smoother_gain * (later_var - pred_var)  10.7 us
    mul x16, other arithmetic, backward(): out_mean = mean_now + smoother_gain * (later_mean - decay_next * mean_now)  10.5 us
    dynamic_update_slice x32, other arithmetic, sequential_smoother(): lax.scan(forward, initial, (grad_all, info_all, decay_all, noise_all, fir...  10.5 us
    div x16, other arithmetic, forward(): var_now = pred_var / (1.0 + info_now * pred_var)  10.5 us
    all_to_all x1, waiting for transfers between devices, shards(): lax.all_to_all(packed, 'tm', split_axis=2, concat_axis=0, tiled=True)  7.51 us
  transfers between devices with their start and end apart: 1, of which 1 were waited for; matrix products, arithmetic and copies ran while one was open for 1% of the time, Pallas kernels for 0%

commit v1 on v0

--- a/solution.py
+++ b/solution.py
@@ -2,6 +2,14 @@
 import jax.numpy as jnp
 from jax import lax
 from jax.sharding import PartitionSpec as P
+
+
+def raise_vectors(axis_k, on_dim, target):
+    v1 = jnp.split(target, lax.axis_size("tm"), axis=on_dim)
+    t_next = jnp.stack(v1, axis=0)
+    return jnp.concatenate(
+        lax.all_to_all(t_next, axis_name="tm", split_axis=0, concat_axis=0), axis=axis_k
+    )
 
 
 def split_path(onehot, values, form):
@@ -119,7 +127,7 @@
     packed = jnp.concatenate(
         [gradient, info_diag[:, None, :], decay[:, None, :], noise_var[:, None, :]], axis=1
     )
-    series = lax.all_to_all(packed, "tm", split_axis=2, concat_axis=0, tiled=True)
+    series = raise_vectors(0, 2, packed)
     local_width = state_total // lax.axis_size("tm")
     prior_here = lax.dynamic_slice_in_dim(
         prior_var, lax.axis_index("tm") * local_width, local_width, 0

time: 154 us -> 137 us (0.89)
  other arithmetic: 63.4 us -> 45.1 us
    unnamed x6 -> x4, other arithmetic: 17.1 us -> 0.01 us
    unnamed x16 -> x28, local copies, waits for them, and re-layouts: 4.97 us -> 10.3 us
    broadcast_in_dim x3 -> x0, local copies, waits for them, and re-layouts: 4.43 us -> none  [the longest x1 1.92 us: shards(): decay[:, None, :]]
where the time goes in v1:
time: 137 us; the launch traced here: 136 us
  other arithmetic  45.1 us (33%)
  local copies, waits for them, and re-layouts  44.3 us (32%)
  matrix products  17.9 us (13%)
  blocking collectives  11.6 us (8%)
  waiting for transfers between devices  7.51 us (5%)
  starting transfers between devices  7.39 us (5%)
  between operations  1.6 us (1%)
    dynamic_slice x48, local copies, waits for them, and re-layouts, sequential_smoother(): lax.scan(forward, initial, (grad_all, info_all, decay_all, noise_all, fir...  20.1 us
    all_to_all x1, blocking collectives, shards(): lax.all_to_all(outgoing, 'tm', split_axis=0, concat_axis=2, tiled=True)  11.6 us
    add x16, other arithmetic, backward(): out_var = var_now + smoother_gain * smoother_gain * (later_var - pred_var)  10.7 us
    mul x16, other arithmetic, backward(): out_mean = mean_now + smoother_gain * (later_mean - decay_next * mean_now)  10.5 us
    dynamic_update_slice x32, other arithmetic, sequential_smoother(): lax.scan(forward, initial, (grad_all, info_all, decay_all, noise_all, fir...  10.3 us
    unnamed x28, local copies, waits for them, and re-layouts  10.3 us
    div x16, other arithmetic, forward(): var_now = pred_var / (1.0 + info_now * pred_var)  10.3 us
    all_to_all x1, waiting for transfers between devices, raise_vectors(): lax.all_to_all(t_next, axis_name='tm', split_axis=0, concat_axis=0)  7.51 us
  transfers between devices with their start and end apart: 1, of which 1 were waited for; matrix products, arithmetic and copies ran while one was open for 1% of the time, Pallas kernels for 0%

profile of v1, /device:TPU:0, one launch (start us, length us, event | category | flops | bytes accessed | tf_op | source)
XLA Modules:
  0.0 136.4 jit_solution(16512214551454644555)
XLA Ops:
  0.6 0.9 copy.102
  1.5 1.4 %convert_bitcast_fusion = bf16[16,512,128]{2,1,0:T(8,128)(2,1)S(1)} fusion(bf16[16,16,128]{2,1,0:T(8,128)(2,1)S(1)} %bitcast.297, s32[512]{0:T(512)} %bitcast.310), kind=kOutput, calls=%fused_computation.65 | convolution fusion | flops 34611200 | bytes 2164736 | tf_op jit(solution)/shard_map/sbk,smkc->smbc/dot_general | solution.py:37
  2.9 7.2 %fusion.23 = f32[512,16,64]{2,1,0:T(8,128)S(1)} fusion(bf16[1,512,64,128]{3,2,1,0:T(8,128)(2,1)} %param.15, bf16[16,512,128]{2,1,0:T(8,128)(2,1)S(1)} %convert_bitcast_fusion), kind=kOutput, calls=%fused_computation.44 | convolution fusion | flops 134217728 | bytes 12582912 | tf_op jit(solution)/shard_map/sbic,smbc->smbi/dot_general | solution.py:40
  11.5 1.0 fusion.33
  12.5 1.1 add_bitcast_fusion
  13.6 2.7 %copy.75 = f32[1,16,512,64]{3,2,1,0:T(8,128)} copy(f32[1,16,512,64]{2,3,1,0:T(8,128)S(1)} %add_bitcast_fusion) | data formatting | bytes 4194304 | tf_op jit(solution)/shard_map/add | solution.py:19
  16.3 2.9 %reshape.252 = f32[1,16,32768]{2,1,0:T(8,128)S(1)} reshape(f32[1,16,512,64]{3,2,1,0:T(8,128)} %copy.75) | data formatting | bytes 4194304 | tf_op jit(solution)/shard_map/reshape | solution.py:44
  19.3 1.8 %multiply_convert_fusion = bf16[1,16,32768]{2,1,0:T(8,128)(2,1)S(1)} fusion(f32[1,16,32768]{2,1,0:T(8,128)} %param.20, f32[1,16,32768]{2,1,0:T(8,128)S(1)} %reshape.252, f32[32768]{0:T(1024)S(1)} %bitcast.299), kind=kLoop, calls=%fused_computation.63 | loop fusion | flops 1572864 | bytes 5373952 | tf_op jit(solution)/shard_map/convert_element_type | solution.py:51
  21.1 2.3 %convert_element_type.58 = bf16[16,512,64]{2,1,0:T(8,128)(2,1)S(1)} reshape(bf16[1,16,32768]{2,1,0:T(8,128)(2,1)S(1)} %multiply_convert_fusion) | data formatting | bytes 2097152 | tf_op jit(solution)/shard_map/convert_element_type | solution.py:51
  23.4 1.5 %fusion.40 = bf16[16,512,64]{1,2,0:T(8,128)(2,1)S(1)} fusion(bf16[16,512,64]{2,1,0:T(8,128)(2,1)S(1)} %convert_element_type.58, s32[512]{0:T(512)S(1)} %bitcast.306, pred[512]{0:T(512)(128)(4,1)S(1)} %iota_compare_fusion.2), kind=kOutput, calls=%fused_computation.67 | convolution fusion | flops 537919488 | bytes 2099712 | tf_op jit(solution)/shard_map/ocd,owdh->owch/dot_general | solution.py:48
  24.9 2.0 %copy.77 = bf16[16,512,64]{2,0,1:T(8,128)(2,1)S(1)} copy(bf16[16,512,64]{1,2,0:T(8,128)(2,1)S(1)} %fusion.40) | data formatting | bytes 2097152 | tf_op jit(solution)/shard_map/reshape.27
  26.9 4.9 %fusion.21 = f32[512,16,128]{2,1,0:T(8,128)S(1)} fusion(bf16[16,512,64]{2,0,1:T(8,128)(2,1)S(1)} %copy.77, bf16[1,512,64,128]{3,2,1,0:T(8,128)(2,1)} %param.15), kind=kOutput, calls=%fused_computation.42 | convolution fusion | flops 134217728 | bytes 13631488 | tf_op jit(solution)/shard_map/sbic,smbi->smbc/dot_general | solution.py:54
  43.4 7.4 %all-to-all-start = ((f32[16,1,19,128]{3,1,2,0:T(1,128)}), f32[16,1,19,128]{3,1,2,0:T(1,128)S(1)}, u32[]{:S(2)}, u32[]{:S(2)}) async-start(f32[16,1,19,128]{3,1,2,0:T(1,128)} %constant_dynamic-update-slice_fusion), calls=%async_computation | async-start | bytes 311296 | tf_op jit(solution)/shard_map/all_to_all | solution.py:11
  50.9 0.8 dynamic_slice.66
  51.6 7.5 %all-to-all-done = f32[16,1,19,128]{3,1,2,0:T(1,128)S(1)} async-done(((f32[16,1,19,128]{3,1,2,0:T(1,128)}), f32[16,1,19,128]{3,1,2,0:T(1,128)S(1)}, u32[]{:S(2)}, u32[]{:S(2)}) %all-to-all-start) | async-done | bytes 155680 | tf_op jit(solution)/shard_map/all_to_all | solution.py:11
  59.2 32.0 %while.38 = (s32[]{:T(128)}, f32[16,128]{1,0:T(8,128)S(1)}, f32[128]{0:T(128)S(1)}, f32[16,16,128]{2,1,0:T(8,128)S(1)}, f32[16,128]{1,0:T(8,128)S(1)}, /*index=5...) while((s32[]{:T(128)}, f32[16,128]{1,0:T(8,128)S(1)}, ...), condition=%wide.region_1.2_spmd.clone, body=%wide.region_0.1_spmd.clone.sunk | while | flops 13315 | bytes 55968 | solution.py:85
  91.3 32.1 %while.39 = (s32[]{:T(128)}, f32[16,128]{1,0:T(8,128)S(1)}, f32[128]{0:T(128)S(1)}, f32[16,16,128]{2,1,0:T(8,128)S(1)}, f32[16,128]{1,0:T(8,128)S(1)}, /*index=5...) while((s32[]{:T(128)}, f32[16,128]{1,0:T(8,128)S(1)}, ...), condition=%wide.region_3.4_spmd.clone, body=%wide.region_2.3_spmd.clone.sunk | while | flops 12420 | bytes 40108 | solution.py:104
  92.6 0.7 fusion.74
  94.6 0.7 fusion.74
  96.6 0.7 fusion.74
  100.6 0.7 fusion.74
  102.7 0.7 fusion.74
  104.7 0.7 fusion.74
  123.4 11.6 %all_to_all.23 = f32[16,17,128]{2,1,0:T(8,128)S(1)} all-to-all(f32[16,17,128]{2,1,0:T(8,128)S(1)} %pad_maximum_fusion), channel_id=1, replica_groups=mesh['group'=2,'tm'=16] {'tm'}, dimensions={0} | all-to-all | bytes 278528 | tf_op jit(solution)/shard_map/all_to_all | solution.py:137
  (211 shorter events, 72.7 us)
Async XLA Ops:
  10.5 1.0 copy-start.1
  16.3 3.0 %copy-start = (f32[1,32768]{1,0:T(1,128)S(1)}, f32[1,32768]{1,0:T(1,128)}, u32[]{:S(2)}) copy-start(f32[1,32768]{1,0:T(1,128)} %param.21) | copy-start | bytes 393220
  32.1 0.7 copy-start.5
  32.8 0.8 copy-start.2
  32.8 0.8 copy-start.3
  32.8 0.8 copy-start.4
  43.4 15.7 %all-to-all-start = ((f32[16,1,19,128]{3,1,2,0:T(1,128)}), f32[16,1,19,128]{3,1,2,0:T(1,128)S(1)}, u32[]{:S(2)}, u32[]{:S(2)}) async-start(f32[16,1,19,128]{3,1,2,0:T(1,128)} %constant_dynamic-update-slice_fusion), calls=%async_computation | async-start | bytes 311296 | tf_op jit(solution)/shard_map/all_to_all | solution.py:11
